TPU v7x, 256 devices: a whole 4x4x8 slice. The times are simulated.
256 devices in a mesh: pair: 64 (over z, y, core), red: 4 (over x).
Axes of the slice: x: 4, y: 4, z: 8, core: 2. Of those that a mesh axis runs over, the one named last changes fastest.
Arguments:
- ints: bfloat16 [4096, 64, 4096], P('pair', 'red'), may hold values from -6 to 6
- block_pairs: int32 [4096, 2], P('pair'), may hold values from 0 to 95
- block_dest: int32 [4096, 1], P('pair'), may hold values from 0 to 63; in each aligned block of 64 rows (0 to 63, 64 to 127, ...) at most 2 rows name the same one
- block_slot: int32 [4096], P('pair'), may hold values from 0 to 3
- occ_density: bfloat16 [96, 64, 64], replicated, may hold values from -0.75 to 0.75
- virt_density: bfloat16 [96, 64, 64], replicated, may hold values from -0.75 to 0.75
- isdf_cols: bfloat16 [96, 64, 256], replicated, may hold values from -0.375 to 0.375
- slab_cols: int32 [128], replicated, may hold values from 0 to 255
Outputs:
- chi_slab: bfloat16 [256, 64, 128], P('pair', 'red')
Inputs may be any that keep to these rules, and one draw needn't show every extreme that they name: `block_dest`: among the 64 blocks of one index of pair (aligned blocks of rows) no owner is named more than 2 times, a bound that some block reaches.
All inputs are finite; a program needn't handle non-finite values.
Results may differ from a plain program's by a relative error of at most 0.015.
Values sent between devices are 32-bit elements; how exact they have to be, the bound alone decides.
A program may use at most 64 MiB of HBM per device.

v0:
```python
import jax
import jax.numpy as jnp
from jax import lax
from jax.sharding import PartitionSpec as P

RB_DEV = 4


def pack_rows(values, owner, slot, npair, capacity):
    onehot = (owner[:, None] == jnp.arange(npair, dtype=jnp.int32)[None, :]).astype(jnp.int32)
    position = jnp.sum(jnp.cumsum(onehot, axis=0) * onehot, axis=1) - 1
    shape = (npair, capacity) + values.shape[1:]
    sendbuf = jnp.zeros(shape, jnp.float32).at[owner, position].set(values)
    labels = jnp.full((npair, capacity), RB_DEV, jnp.int32).at[owner, position].set(slot)
    return (sendbuf, labels)


def unpack_rows(received, labels):
    count = received.shape[0] * received.shape[1]
    inner = received.shape[2:]
    flat = received.reshape((count,) + inner)
    flat_labels = labels.reshape(count)
    slots = []
    for target in range(RB_DEV):
        keep = (flat_labels == target)[:, None, None]
        slots.append(jnp.sum(jnp.where(keep, flat, jnp.float32(0.0)), axis=0))
    return jnp.stack(slots, axis=0)


def shards(
    ints, block_pairs, block_dest, block_slot, occ_density, virt_density, isdf_cols, slab_cols
):
    npair = lax.axis_size("pair")
    blocks, quarter, width = ints.shape
    basis = occ_density.shape[1]
    rsize = width // basis
    ncols = slab_cols.shape[0]
    group = lax.axis_index("red")
    sel = jnp.take(isdf_cols, slab_cols, axis=2)
    occ_side = jnp.einsum(
        "amn,amq->anq", occ_density, sel, preferred_element_type=jnp.float32
    ).astype(jnp.bfloat16)
    virt_rows = lax.dynamic_slice_in_dim(virt_density, group * quarter, quarter, 1)

    def one_block(args):
        ints_b, pair = args
        occ_b = occ_side[pair[0]].astype(jnp.float32)
        sel_b = sel[pair[1]].astype(jnp.float32)
        factor = (
            (occ_b[:, None, :] * sel_b[None, :, :])
            .astype(jnp.bfloat16)
            .reshape(basis * basis, ncols)
        )
        virt_b = virt_rows[pair[1]]
        half = lax.dot_general(
            ints_b, virt_b, (((0,), (0,)), ((), ())), preferred_element_type=jnp.float32
        )
        half = half.astype(jnp.bfloat16).reshape(rsize, basis * basis)
        return jnp.dot(half, factor, preferred_element_type=jnp.float32)

    parts = lax.map(one_block, (ints, block_pairs))
    owner = block_dest[:, 0]
    capacity = 2 * blocks // npair
    sendbuf, labels = pack_rows(parts, owner, block_slot, npair, capacity)
    received = lax.all_to_all(sendbuf, "pair", split_axis=0, concat_axis=0, tiled=True)
    got_labels = lax.all_to_all(labels, "pair", split_axis=0, concat_axis=0, tiled=True)
    local_rows = unpack_rows(received, got_labels)
    result = lax.psum_scatter(local_rows, "red", scatter_dimension=1, tiled=True)
    return result.astype(jnp.bfloat16)


def solution(mesh):
    return jax.shard_map(
        shards,
        mesh=mesh,
        in_specs=(
            P("pair", "red", None),
            P("pair", None),
            P("pair", None),
            P("pair"),
            P(),
            P(),
            P(),
            P(),
        ),
        out_specs=P("pair", "red", None),
        check_vma=False,
    )
```

profile of v0, /device:TPU:2, one launch (start us, length us, event | category | flops | bytes accessed | tf_op | source)
XLA Modules:
  0.0 988.9 jit_solution(8677140628432773869)
XLA Ops:
  9.0 5.8 scatter_fusion
  15.4 12.4 %all-to-all-start = ((s32[64,1,2]{2,1,0:T(1,128)}), s32[64,1,2]{2,1,0:T(1,128)}, u32[]{:S(2)}, u32[]{:S(2)}) async-start(s32[64,1,2]{2,1,0:T(1,128)} %copy.56), calls=%async_computation | async-start | bytes 65536 | tf_op jit(solution)/shard_map/all_to_all | solution.py:66
  29.5 7.0 copy.60
  36.5 4.3 gather_fusion
  42.7 3.2 copy.61
  45.9 4.0 copy.62
  49.9 3.2 fusion.6
  53.0 787.2 %while.10 = (s32[]{:T(128)}, f32[64,64,128]{2,1,0:T(8,128)}, bf16[64,16,4096]{2,1,0:T(8,128)(2,1)}, s32[64,2]{0,1:T(2,128)S(1)}, bf16[96,16,64]{2,1,0:T(8,128)(2...) while((s32[]{:T(128)}, f32[64,64,128]{2,1,0:T(8,128)}, ...), condition=%wide.region_4.5_spmd, body=%wide.region_3.4_spmd.sunk | while | flops 76824584 | bytes 5575897 | solution.py:61
  156.6 2.0 convolution_convert_fusion.3
  205.8 2.0 convolution_convert_fusion.3
  304.1 2.0 convolution_convert_fusion.3
  316.4 2.0 convolution_convert_fusion.3
  353.3 2.0 convolution_convert_fusion.3
  377.9 2.0 convolution_convert_fusion.3
  500.9 2.0 convolution_convert_fusion.3
  513.2 2.0 convolution_convert_fusion.3
  550.1 2.0 convolution_convert_fusion.3
  611.6 2.0 convolution_convert_fusion.3
  624.0 2.0 convolution_convert_fusion.3
  673.2 2.0 convolution_convert_fusion.3
  685.5 2.0 convolution_convert_fusion.3
  710.1 2.0 convolution_convert_fusion.3
  722.4 2.0 convolution_convert_fusion.3
  734.7 2.0 convolution_convert_fusion.3
  771.6 2.0 convolution_convert_fusion.3
  783.9 2.0 convolution_convert_fusion.3
  840.3 2.5 broadcast_in_dim.66
  842.8 9.3 scatter_fusion.1
  852.1 10.6 %all-to-all-start.1 = ((f32[64,2,64,128]{3,2,1,0:T(8,128)}), f32[64,2,64,128]{3,2,1,0:T(8,128)}, u32[]{:S(2)}, u32[]{:S(2)}) async-start(f32[64,2,64,128]{3,2,1,0:T(8,128)} %scatter_fusion.1), calls=%async_computation.1 | async-start | bytes 8388608 | tf_op jit(solution)/shard_map/all_to_all | solution.py:65
  864.0 94.9 %all-to-all-done.1 = f32[64,2,64,128]{3,2,1,0:T(8,128)} async-done(((f32[64,2,64,128]{3,2,1,0:T(8,128)}), f32[64,2,64,128]{3,2,1,0:T(8,128)}, u32[]{:S(2)}, u32[]{:S(2)}) %all-to-all-start.1) | async-done | bytes 4194336 | tf_op jit(solution)/shard_map/all_to_all | solution.py:65
  958.9 3.8 select_reduce_fusion.3
  963.3 17.4 %reduce-scatter.2.cloned.1.call-done = f32[4,16,128]{2,1,0:T(8,128)} async-done(((f32[4,64,128]{2,1,0:T(8,128)}), f32[4,16,128]{2,1,0:T(8,128)}) %reduce-scatter.2.cloned.1.call-update) | async-done | bytes 32784 | tf_op jit(solution)/shard_map/reduce_scatter | solution.py:68
  (524 shorter events, 535.7 us)
Async XLA Ops:
  6.5 22.6 %copy-start = (bf16[96,64,64]{0,2,1:T(8,128)(2,1)S(1)}, bf16[96,64,64]{0,2,1:T(8,128)(2,1)}, u32[]{:S(2)}) copy-start(bf16[96,64,64]{0,2,1:T(8,128)(2,1)} %param.15) | copy-start | bytes 2359300
  15.4 836.7 %all-to-all-start = ((s32[64,1,2]{2,1,0:T(1,128)}), s32[64,1,2]{2,1,0:T(1,128)}, u32[]{:S(2)}, u32[]{:S(2)}) async-start(s32[64,1,2]{2,1,0:T(1,128)} %copy.56), calls=%async_computation | async-start | bytes 65536 | tf_op jit(solution)/shard_map/all_to_all | solution.py:66
  49.9 3.2 copy-start.2
  840.3 2.5 copy-start.1
  852.1 106.8 %all-to-all-start.1 = ((f32[64,2,64,128]{3,2,1,0:T(8,128)}), f32[64,2,64,128]{3,2,1,0:T(8,128)}, u32[]{:S(2)}, u32[]{:S(2)}) async-start(f32[64,2,64,128]{3,2,1,0:T(8,128)} %scatter_fusion.1), calls=%async_computation.1 | async-start | bytes 8388608 | tf_op jit(solution)/shard_map/all_to_all | solution.py:65
  862.7 118.1 %reduce-scatter.2.cloned.1.call-start = ((), (), s32[]{:S(2)}) async-start(), calls=%async_computation.3 | async-start | bytes 163840 | tf_op jit(solution)/shard_map/reduce_scatter | solution.py:68
Sparse Core Ops, SparseCore 0:
  963.5 17.2 reduce-scatter.1
where the time goes:
time: 1010 us; the launch traced here: 989 us
  local copies, waits for them, and re-layouts  278 us (28%)
  matrix products  260 us (26%)
  loops' own time  225 us (22%)
  waiting for transfers between devices  112 us (11%)
  other arithmetic  77.4 us (8%)
  starting transfers between devices  23 us (2%)
  between operations  13.5 us (1%)
    another operation x1, loops' own time, shards(): parts = lax.map(one_block, (ints, block_pairs))  225 us
    dot_general x64, matrix products, one_block(): lax.dot_general(ints_b, virt_b, (((0,), (0,)), ((), ())), preferred_eleme...  131 us
    dot_general x64, matrix products, one_block(): return jnp.dot(half, factor, preferred_element_type=jnp.float32)  126 us
    reshape x64, local copies, waits for them, and re-layouts, one_block(): half = half.astype(jnp.bfloat16).reshape(rsize, basis * basis)  104 us
    convert_element_type x64, local copies, waits for them, and re-layouts, one_block(): half = half.astype(jnp.bfloat16).reshape(rsize, basis * basis)  96.9 us
    all_to_all x1, waiting for transfers between devices, shards(): lax.all_to_all(sendbuf, 'pair', split_axis=0, concat_axis=0, tiled=True)  94.9 us
    mul x64, other arithmetic, one_block(): occ_b[:, None, :] * sel_b[None, :, :]  47.9 us
    slice x64, local copies, waits for them, and re-layouts, one_block(): occ_b = occ_side[pair[0]].astype(jnp.float32)  33.9 us
  transfers between devices with their start and end apart: 3, of which 2 were waited for; matrix products, arithmetic and copies ran while one was open for 61% of the time, Pallas kernels for 0%

commit v1 on v0

v1 whole, which is shorter than its diff:
```python
import functools

import jax
import jax.numpy as jnp
from jax import lax
from jax.experimental import pallas as pl
from jax.experimental.pallas import tpu as pltpu
from jax.sharding import PartitionSpec as P

MESH = pl.DeviceIdType.MESH
BF, F32 = jnp.bfloat16, jnp.float32

NB = 64
LAM = 16
BA = 64
NAB = 96
NQ = 128
NCAND = 256
PQ = 16
NX, NY, NZ = 4, 4, 8
SLOTS = 4
CB = 8
NCH = NB // CB
YC = 2
PC = PQ // YC


def kernel(
    ints_hbm, pairs_smem, pairs_ref, dest_ref, slot_ref, slab_ref, occ_hbm, virt_hbm, isdf_hbm,
    out_ref,
    ints, occ_t, virt_t, isdf, sel, dens, vdens, wbd, vside,
    parts, rxo, rxn, kown, koth, coreacc, dense, ryo, ryn, zbuf, zrecv, outf,
    load_sem, ints_sem, xs, xr, ks, kr, ys, yr, zs, zr,
):
    pair = lax.axis_index("pair")
    red = lax.axis_index("red")
    core = lax.rem(pair, 2)
    y = lax.rem(pair // 2, NY)
    z = pair // (2 * NY)

    def dev(zz, yy, cc, rr):
        return ((zz * NY + yy) * 2 + cc, rr)

    x_opp, x_r, x_l = lax.rem(red + 2, NX), lax.rem(red + 1, NX), lax.rem(red + 3, NX)
    y_opp, y_r, y_l = lax.rem(y + 2, NY), lax.rem(y + 1, NY), lax.rem(y + 3, NY)
    right_x, left_x = dev(z, y, core, x_r), dev(z, y, core, x_l)
    right_y, left_y = dev(z, y_r, core, red), dev(z, y_l, core, red)
    other = dev(z, y, 1 - core, red)

    loads = [
        pltpu.make_async_copy(isdf_hbm, isdf, load_sem.at[0]),
        pltpu.make_async_copy(virt_hbm.at[pl.ds(red * (LAM * BA), LAM * BA)], virt_t, load_sem.at[1]),
        pltpu.make_async_copy(occ_hbm, occ_t, load_sem.at[2]),
    ]
    for c in loads:
        c.start()

    def ints_copy(k):
        return pltpu.make_async_copy(
            ints_hbm.at[pl.ds(k * CB, CB)], ints.at[pl.ds(k * CB, CB)], ints_sem.at[k]
        )

    for k in range(NCH):
        ints_copy(k).start()

    barrier = pltpu.get_barrier_semaphore()
    peers = [right_x, left_x, right_y, left_y, other]
    peers += [dev(lax.rem(z + h, NZ), y, core, red) for h in range(1, NZ)]
    for d in peers:
        pl.semaphore_signal(barrier, inc=1, device_id=d, device_id_type=MESH)

    pick = (lax.broadcasted_iota(jnp.int32, (NCAND, NQ), 0) == slab_ref[...]).astype(F32).astype(BF)

    def one_hot_rows(row):
        wide = jnp.concatenate([pairs_ref[row : row + 1, :], jnp.full((1, 128 - NB), -1, jnp.int32)], axis=1)
        t = (lax.broadcasted_iota(jnp.int32, (128, 128), 0) == wide).astype(F32)
        return jnp.transpose(t)[:NB, :NAB].astype(BF)

    hot_i, hot_j = one_hot_rows(0), one_hot_rows(1)
    keys = dest_ref[...] * SLOTS + slot_ref[...]
    kown[...] = jnp.broadcast_to(jnp.concatenate([keys, keys], axis=1), (8, 128))

    loads[0].wait()
    rows = 512

    def sel_step(i, carry):
        at = pl.ds(pl.multiple_of(i * rows, rows), rows)
        got = jnp.dot(isdf[at, :], pick, preferred_element_type=F32).astype(BF)
        sel[pl.ds(i * (rows // BA), rows // BA)] = got.reshape(rows // BA, BA, NQ)
        return carry

    lax.fori_loop(0, NAB * BA // rows, sel_step, 0)

    low = lax.broadcasted_iota(jnp.int32, (NB, 128), 1) < BA

    def gathered(hot, src, dst, count):
        for tile in range(count * BA // 512):
            t = lax.dot_general(
                hot, src[tile * 512 : (tile + 1) * 512, :], (((1,), (1,)), ((), ())),
                preferred_element_type=F32,
            )
            for j in range(4):
                both = t[:, j * 128 : (j + 1) * 128]
                turned = pltpu.roll(both, BA, 1)
                m = tile * 8 + j * 2
                dst[pl.ds(m, NB, stride=count), :] = jnp.where(low, both, turned)
                dst[pl.ds(m + 1, NB, stride=count), :] = jnp.where(low, turned, both)

    loads[1].wait()
    gathered(hot_j, virt_t, vdens, LAM)
    loads[2].wait()
    gathered(hot_i, occ_t, dens, BA)

    top = lax.broadcasted_iota(jnp.int32, (2 * BA, NQ), 0) < BA

    def side_step(b, carry):
        first, second = pairs_smem[0, b], pairs_smem[1, b]
        sel_i, sel_j = sel[first], sel[second]
        d = dens[pl.ds(pl.multiple_of(b * BA, BA), BA), :].astype(BF)
        occ = lax.dot_general(d, sel_i, (((0,), (0,)), ((), ())), preferred_element_type=F32)
        wbd[b] = jnp.concatenate([jnp.where(top, occ, 0.0), jnp.where(top, 0.0, occ)], axis=1).astype(BF)
        v = vdens[pl.ds(pl.multiple_of(b * LAM, LAM), LAM), :BA].astype(BF)
        vside[b] = jnp.dot(v, sel_j, preferred_element_type=F32)
        return carry

    lax.fori_loop(0, NB, side_step, 0, unroll=4)

    def block_step(b, carry):
        x = ints[b]
        lhs = jnp.concatenate([x[:, i * 128 : (i + 1) * 128] for i in range(32)], axis=0)
        t = jnp.dot(lhs, wbd[b], preferred_element_type=F32)
        v = vside[b]
        vv = jnp.concatenate([v, v], axis=1)
        t = t.reshape(32, LAM, 2 * NQ) * vv[None]
        part = jnp.sum(t, axis=1)
        for r in range(NX):
            for lo in range(2):
                parts[pl.ds((r * PQ + lo * 8) * NB + b, 8, stride=NB), :] = part[r * 8 : r * 8 + 8, lo * NQ : (lo + 1) * NQ]
        return carry

    def remote(src, dst, send, recv, to):
        return pltpu.make_async_remote_copy(
            src_ref=src, dst_ref=dst, send_sem=send, recv_sem=recv, device_id=to, device_id_type=MESH
        )

    parts4 = parts.reshape(NX, PQ, NB, NQ)
    H = PQ // 2

    def x_copy(i, k):
        at = pl.ds(pl.multiple_of(k * CB, CB), CB)
        lo, hi = pl.ds(0, H), pl.ds(H, H)
        src, dst, to = {
            0: ((x_opp, lo, at), rxo.at[0, :, at], right_x),
            1: ((x_opp, hi, at), rxo.at[1, :, at], left_x),
            2: ((x_r, hi, at), rxn.at[0, hi, at], right_x),
            3: ((x_l, lo, at), rxn.at[1, lo, at], left_x),
            4: ((x_r, lo, at), rxn.at[0, lo, at], right_x),
            5: ((x_l, hi, at), rxn.at[1, hi, at], left_x),
            6: ((red, slice(None), at), coreacc.at[:, at], other),
        }[i]
        return remote(parts4.at[src], dst, xs.at[i, k], xr.at[i, k], to)

    pl.semaphore_wait(barrier, len(peers))
    key_copy = remote(kown, koth, ks.at[0], kr.at[0], other)
    key_copy.start()

    def chunk_step(t, carry):
        @pl.when(t < NCH)
        def _():
            ints_copy(t).wait()
            lax.fori_loop(t * CB, (t + 1) * CB, block_step, 0)
            for i in range(4):
                x_copy(i, t).start()

        @pl.when((t >= 1) & (t < NCH + 1))
        def _():
            k = t - 1
            at = pl.ds(pl.multiple_of(k * CB, CB), CB)
            x_copy(0, k).wait_recv()
            parts4[x_r, 0:H, at] += rxo[0, :, at]
            x_copy(4, k).start()
            x_copy(1, k).wait_recv()
            parts4[x_l, H:PQ, at] += rxo[1, :, at]
            x_copy(5, k).start()

        @pl.when(t >= 2)
        def _():
            k = t - 2
            at = pl.ds(pl.multiple_of(k * CB, CB), CB)
            for i in (2, 3, 4, 5):
                x_copy(i, k).wait_recv()
            parts4[red, :, at] += rxn[0, :, at] + rxn[1, :, at]
            x_copy(6, k).start()

        return carry

    lax.fori_loop(0, NCH + 2, chunk_step, 0)

    key_copy.wait()
    lane = lax.broadcasted_iota(jnp.int32, (1, 2 * NB), 1)
    both_keys = jnp.where(lane < NB, kown[0:1, :], koth[0:1, :])
    row = lax.broadcasted_iota(jnp.int32, (NY * NZ * SLOTS, 2 * NB), 0)
    ry, rz, rs = row // (NZ * SLOTS), (row // SLOTS) % NZ, row % SLOTS
    code = (((rz * NY) + ry) * 2 + core) * SLOTS + rs
    place = (code == both_keys).astype(F32).astype(BF)
    place2 = jnp.concatenate([place, place], axis=1)

    for k in range(NCH):
        x_copy(6, k).wait_recv()
    for p in range(0, PQ, 2):
        own = jnp.concatenate([parts4[red, p], parts4[red, p + 1]], axis=1)
        oth = jnp.concatenate([coreacc[p], coreacc[p + 1]], axis=1)
        both = jnp.concatenate([own, oth], axis=0)
        high = both.astype(BF)
        rest = (both - high.astype(F32)).astype(BF)
        d = jnp.dot(place2, jnp.concatenate([high, rest], axis=0), preferred_element_type=F32)
        dense[p] = d[:, :NQ].reshape(NY, NZ * SLOTS, NQ)
        dense[p + 1] = d[:, NQ:].reshape(NY, NZ * SLOTS, NQ)

    Q = PC // 2

    def y_copy(i, c):
        lo, hi = pl.ds(c * PC, Q), pl.ds(c * PC + Q, Q)
        src, dst, to = {
            0: ((lo, y_opp), ryo.at[0, c], right_y),
            1: ((hi, y_opp), ryo.at[1, c], left_y),
            2: ((hi, y_r), ryn.at[0, hi], right_y),
            3: ((lo, y_l), ryn.at[1, lo], left_y),
            4: ((lo, y_r), ryn.at[0, lo], right_y),
            5: ((hi, y_l), ryn.at[1, hi], left_y),
        }[i]
        return remote(dense.at[src], dst, ys.at[i, c], yr.at[i, c], to)

    def z_copy(h, c):
        zz = lax.rem(z + h, NZ)
        return remote(
            zbuf.at[c, zz], zrecv.at[c, z], zs.at[c, h], zr.at[c, z], dev(zz, y, core, red)
        )

    def z_wait(h, c):
        zz = lax.rem(z + h, NZ)
        remote(zbuf.at[c, zz], zrecv.at[c, zz], zs.at[c, h], zr.at[c, zz], other).wait_recv()

    zflat = zbuf.reshape(YC, NZ * SLOTS * PC, NQ)
    for c in range(YC):
        for i in range(4):
            y_copy(i, c).start()
    for c in range(YC):
        y_copy(0, c).wait_recv()
        dense[c * PC : c * PC + Q, y_r] += ryo[0, c]
        y_copy(4, c).start()
        y_copy(1, c).wait_recv()
        dense[c * PC + Q : (c + 1) * PC, y_l] += ryo[1, c]
        y_copy(5, c).start()
    for c in range(YC):
        for i in (2, 3, 4, 5):
            y_copy(i, c).wait_recv()
        for i in range(PC):
            p = c * PC + i
            zflat[c, pl.ds(i, NZ * SLOTS, stride=PC), :] = dense[p, y] + ryn[0, p] + ryn[1, p]
        for h in range(1, NZ):
            z_copy(h, c).start()
    for c in range(YC):
        for h in range(1, NZ):
            z_wait(h, c)
        total = zbuf[c, z]
        for h in range(1, NZ):
            total = total + zrecv[c, lax.rem(z + h, NZ)]
        outf[pl.ds(c, SLOTS * PC, stride=2), :] = total
    out_ref[...] = outf[...].astype(BF).reshape(SLOTS, PQ, NQ)

    def finish(k, carry):
        for i in range(7):
            x_copy(i, k).wait_send()
        return carry

    lax.fori_loop(0, NCH, finish, 0)
    for c in range(YC):
        for i in range(6):
            y_copy(i, c).wait_send()
        for h in range(1, NZ):
            z_copy(h, c).wait_send()


def shards(
    ints, block_pairs, block_dest, block_slot, occ_density, virt_density, isdf_cols, slab_cols
):
    hbm = pl.BlockSpec(memory_space=pl.ANY)
    vmem = pl.BlockSpec(memory_space=pltpu.VMEM)
    smem = pl.BlockSpec(memory_space=pltpu.SMEM)
    dma = pltpu.SemaphoreType.DMA
    pairs_t = block_pairs.T
    return pl.pallas_call(
        kernel,
        out_shape=jax.ShapeDtypeStruct((SLOTS, PQ, NQ), BF),
        in_specs=[hbm, smem, vmem, vmem, vmem, vmem, hbm, hbm, hbm],
        out_specs=vmem,
        scratch_shapes=[
            pltpu.VMEM((NB, LAM, BA * BA), BF),
            pltpu.VMEM((BA * BA, NAB), BF),
            pltpu.VMEM((LAM * BA, NAB), BF),
            pltpu.VMEM((NAB * BA, NCAND), BF),
            pltpu.VMEM((NAB, BA, NQ), BF),
            pltpu.VMEM((NB * BA, 2 * BA), F32),
            pltpu.VMEM((NB * LAM, 2 * BA), F32),
            pltpu.VMEM((NB, 2 * BA, 2 * NQ), BF),
            pltpu.VMEM((NB, LAM, NQ), F32),
            pltpu.VMEM((NX * PQ * NB, NQ), F32),
            pltpu.VMEM((2, PQ // 2, NB, NQ), F32),
            pltpu.VMEM((2, PQ, NB, NQ), F32),
            pltpu.VMEM((8, 128), jnp.int32),
            pltpu.VMEM((8, 128), jnp.int32),
            pltpu.VMEM((PQ, NB, NQ), F32),
            pltpu.VMEM((PQ, NY, NZ * SLOTS, NQ), F32),
            pltpu.VMEM((2, YC, PC // 2, NZ * SLOTS, NQ), F32),
            pltpu.VMEM((2, PQ, NZ * SLOTS, NQ), F32),
            pltpu.VMEM((YC, NZ, SLOTS * PC, NQ), F32),
            pltpu.VMEM((YC, NZ, SLOTS * PC, NQ), F32),
            pltpu.VMEM((SLOTS * PQ, NQ), F32),
            dma((3,)),
            dma((NCH,)),
            dma((7, NCH)),
            dma((7, NCH)),
            dma((1,)),
            dma((1,)),
            dma((6, YC)),
            dma((6, YC)),
            dma((YC, NZ)),
            dma((YC, NZ)),
        ],
        compiler_params=pltpu.CompilerParams(
            collective_id=0, has_side_effects=True, vmem_limit_bytes=56 * 1024 * 1024
        ),
        cost_estimate=pl.CostEstimate(flops=3_000_000_000, bytes_accessed=14_000_000, transcendentals=0),
    )(
        ints,
        pairs_t,
        pairs_t,
        block_dest.reshape(1, NB),
        block_slot.reshape(1, NB),
        slab_cols.reshape(1, NQ),
        occ_density.transpose(1, 2, 0).reshape(BA * BA, NAB),
        virt_density.transpose(1, 2, 0).reshape(BA * BA, NAB),
        isdf_cols.reshape(NAB * BA, NCAND),
    )


def solution(mesh):
    return jax.shard_map(
        shards,
        mesh=mesh,
        in_specs=(
            P("pair", "red", None),
            P("pair", None),
            P("pair", None),
            P("pair"),
            P(),
            P(),
            P(),
            P(),
        ),
        out_specs=P("pair", "red", None),
        check_vma=False,
    )
```

time: 1010 us -> 75 us (0.07); the launches traced: 989 us -> 74.5 us
  local copies, waits for them, and re-layouts: 278 us -> 1.32 us
  matrix products: 260 us -> 0 us
  loops' own time: 225 us -> 0 us
  waiting for transfers between devices: 112 us -> 0 us
  other arithmetic: 77.4 us -> 0 us
  Pallas kernels: 0 us -> 73.2 us
  starting transfers between devices: 23 us -> 0 us
  between operations: 13.5 us -> 0.01 us
    dot_general x129 -> x0, matrix products: 260 us -> none  [the longest x64 131 us: one_block(): lax.dot_general(ints_b, virt_b, (((0,), (0,)), ((), ())), preferred_eleme...]
    another operation x1 -> x0, loops' own time: 225 us -> none  [shards(): parts = lax.map(one_block, (ints, block_pairs))]
    reshape x64 -> x0, local copies, waits for them, and re-layouts: 104 us -> none  [one_block(): half = half.astype(jnp.bfloat16).reshape(rsize, basis * basis)]
    convert_element_type x64 -> x0, local copies, waits for them, and re-layouts: 96.9 us -> none  [one_block(): half = half.astype(jnp.bfloat16).reshape(rsize, basis * basis)]
    all_to_all x2 -> x0, waiting for transfers between devices: 94.9 us -> none  [the longest x1 94.9 us: shards(): lax.all_to_all(sendbuf, 'pair', split_axis=0, concat_axis=0, tiled=True)]
    pallas_call x0 -> x1, Pallas kernels: none -> 73.2 us  [shards(): pl.pallas_call(kernel, out_shape=jax.ShapeDtypeStruct((SLOTS, PQ, NQ), BF...]
    mul x64 -> x0, other arithmetic: 47.9 us -> none  [one_block(): occ_b[:, None, :] * sel_b[None, :, :]]
    slice x64 -> x0, local copies, waits for them, and re-layouts: 33.9 us -> none  [one_block(): occ_b = occ_side[pair[0]].astype(jnp.float32)]
  transfers between devices with their start and end apart: 3 -> 0, of which waited for: 2 -> 0; matrix products, arithmetic and copies ran while one was open for 61% -> 0% of each run, Pallas kernels for 0% -> 0%
where the time goes in v1:
time: 75 us; the launch traced here: 74.5 us
  Pallas kernels  73.2 us (98%)
  local copies, waits for them, and re-layouts  1.32 us (2%)
    pallas_call x1, Pallas kernels, shards(): pl.pallas_call(kernel, out_shape=jax.ShapeDtypeStruct((SLOTS, PQ, NQ), BF...  73.2 us

profile of v1, /device:TPU:2, one launch (start us, length us, event | category | flops | bytes accessed | tf_op | source)
XLA Modules:
  0.0 74.5 jit_solution(18333200654392720527)
XLA Ops:
  0.0 73.2 %shard_map.82 = bf16[4,16,128]{2,1,0:T(8,128)(2,1)} custom-call(bf16[64,16,4096]{2,1,0:T(8,128)(2,1)} %ints_hbm.1, s32[2,64]{1,0:T(2,128)} %bitcast.14, s32[2,64]{1,0:T(2,128)} %bitcast.15, s32[1,64]{1,0:T(1,128)} %bitcast.16, s32[1,64]{1,0:T(1,128)} %bitcast.17, s32[1,128]{1,0:T(1,128)} %bitcast.18, bf16[4096,96]{1,0:T(8,128)(2,1)} %bitcast.12, ...), custom_call_target="tpu_custom_call" | custom-call | flops 3000000000 | bytes 14000000 | tf_op jit(solution)/shard_map/pallas_call | solution.py:293
  73.2 1.3 %copy.10 = bf16[4,16,128]{2,1,0:T(8,128)(2,1)} copy(bf16[4,16,128]{2,1,0:T(8,128)(2,1)} %shard_map.82) | data formatting | bytes 32768

commit v2 on v1

v2 whole, which is shorter than its diff:
```python
import functools

import jax
import jax.numpy as jnp
from jax import lax
from jax.experimental import pallas as pl
from jax.experimental.pallas import tpu as pltpu
from jax.sharding import PartitionSpec as P

MESH = pl.DeviceIdType.MESH
BF, F32 = jnp.bfloat16, jnp.float32

NB = 64
LAM = 16
BA = 64
NAB = 96
NQ = 128
NCAND = 256
PQ = 16
NX, NY, NZ = 4, 4, 8
SLOTS = 4
CB = 8
NCH = NB // CB
GROUPS = ((0, 8), (8, 4), (12, 4))
NG = len(GROUPS)
CHUNKS = (8, 4, 1)
KEYS = NZ * SLOTS


def kernel(
    ints_hbm, pairs_smem, pairs_ref, dest_ref, slot_ref, slab_ref, occ_hbm, virt_hbm, isdf_hbm,
    out_ref,
    ints, occ_t, virt_t, isdf, dflat, vflat, dens, vdens, wbd, vside,
    parts, rxo, rxn, kown, koth, coreacc, dense, ryn, zbuf, zrecv, outf,
    load_sem, ints_sem, xs, xr, cs, cr, ks, kr, ys, yr, zs, zr,
):
    pair = lax.axis_index("pair")
    red = lax.axis_index("red")
    core = lax.rem(pair, 2)
    y = lax.rem(pair // 2, NY)
    z = pair // (2 * NY)

    def dev(zz, yy, cc, rr):
        return ((zz * NY + yy) * 2 + cc, rr)

    x_opp, x_r, x_l = lax.rem(red + 2, NX), lax.rem(red + 1, NX), lax.rem(red + 3, NX)
    right_x, left_x = dev(z, y, core, x_r), dev(z, y, core, x_l)
    other = dev(z, y, 1 - core, red)

    half = NAB // 2
    loads = [
        pltpu.make_async_copy(virt_hbm.at[pl.ds(red * (LAM * BA), LAM * BA)], virt_t, load_sem.at[0]),
        pltpu.make_async_copy(occ_hbm, occ_t, load_sem.at[1]),
        pltpu.make_async_copy(isdf_hbm.at[pl.ds(0, half)], isdf.at[pl.ds(0, half)], load_sem.at[2]),
        pltpu.make_async_copy(isdf_hbm.at[pl.ds(half, half)], isdf.at[pl.ds(half, half)], load_sem.at[3]),
    ]
    for c in loads:
        c.start()

    def ints_copy(k):
        return pltpu.make_async_copy(
            ints_hbm.at[pl.ds(k * CB, CB)], ints.at[pl.ds(k * CB, CB)], ints_sem.at[k]
        )

    ints_copy(0).start()

    barrier = pltpu.get_barrier_semaphore()
    peers = [right_x, left_x, other]
    peers += [dev(z, lax.rem(y + h, NY), core, red) for h in range(1, NY)]
    peers += [dev(lax.rem(z + h, NZ), y, core, red) for h in range(1, NZ)]
    for d in peers:
        pl.semaphore_signal(barrier, inc=1, device_id=d, device_id_type=MESH)

    pick = (lax.broadcasted_iota(jnp.int32, (NCAND, NQ), 0) == slab_ref[...]).astype(F32).astype(BF)

    def one_hot_rows(row):
        wide = jnp.concatenate([pairs_ref[row : row + 1, :], jnp.full((1, 128 - NB), -1, jnp.int32)], axis=1)
        t = (lax.broadcasted_iota(jnp.int32, (128, 128), 0) == wide).astype(F32)
        return jnp.transpose(t)[:NB, :NAB].astype(BF)

    hot_i, hot_j = one_hot_rows(0), one_hot_rows(1)
    keys = dest_ref[...] * SLOTS + slot_ref[...]
    kown[...] = jnp.broadcast_to(jnp.concatenate([keys, keys], axis=1), (8, 128))

    low = lax.broadcasted_iota(jnp.int32, (CB, 128), 1) < BA

    def gathered(hot, src, dst):
        for at in range(0, dst.shape[1], 512):
            dst[:, at : at + 512] = lax.dot_general(
                hot, src[at : at + 512, :], (((1,), (1,)), ((), ())), preferred_element_type=F32
            )

    def turned(flat, t, dst, count):
        at = pl.ds(pl.multiple_of(t * CB, CB), CB)
        for m in range(0, count, 2):
            both = flat[at, m * BA : (m + 2) * BA]
            back = pltpu.roll(both, BA, 1)
            dst[pl.ds(m, CB, stride=count), :] = jnp.where(low, both, back)
            dst[pl.ds(m + 1, CB, stride=count), :] = jnp.where(low, back, both)

    loads[0].wait()
    gathered(hot_j, virt_t, vflat)
    loads[1].wait()
    gathered(hot_i, occ_t, dflat)

    top = lax.broadcasted_iota(jnp.int32, (2 * BA, NQ), 0) < BA

    def sides(t):
        turned(vflat, t, vdens, LAM)
        turned(dflat, t, dens, BA)
        ids = [(pairs_smem[0, t * CB + i], pairs_smem[1, t * CB + i]) for i in range(CB)]
        cols = jnp.concatenate([isdf[a] for both in ids for a in both], axis=0)
        sel = jnp.dot(cols, pick, preferred_element_type=F32).astype(BF)
        for i in range(CB):
            b = t * CB + i
            sel_i, sel_j = sel[2 * i * BA : (2 * i + 1) * BA], sel[(2 * i + 1) * BA : (2 * i + 2) * BA]
            d = dens[i * BA : (i + 1) * BA, :].astype(BF)
            occ = lax.dot_general(d, sel_i, (((0,), (0,)), ((), ())), preferred_element_type=F32)
            wbd[b] = jnp.concatenate([jnp.where(top, occ, 0.0), jnp.where(top, 0.0, occ)], axis=1).astype(BF)
            v = vdens[i * LAM : (i + 1) * LAM, :BA].astype(BF)
            vside[b] = jnp.dot(v, sel_j, preferred_element_type=F32)

    sub = lax.broadcasted_iota(jnp.int32, (8, 2 * NQ), 0)

    def block_step(b, carry):
        x = ints[b]
        lhs = jnp.concatenate([x[:, i * 128 : (i + 1) * 128] for i in range(32)], axis=0)
        t = jnp.dot(lhs, wbd[b], preferred_element_type=F32)
        v = vside[b]
        v_lo = jnp.concatenate([v[:8], v[:8]], axis=1)
        v_hi = jnp.concatenate([v[8:], v[8:]], axis=1)
        tiles = [t[16 * p : 16 * p + 8] * v_lo + t[16 * p + 8 : 16 * p + 16] * v_hi for p in range(32)]
        for bit in range(3):
            mask = (sub & (1 << bit)) == 0
            tiles = [
                jnp.where(mask, a, c) + pltpu.roll(jnp.where(mask, c, a), 1 << bit, 0)
                for a, c in zip(tiles[0::2], tiles[1::2])
            ]
        for r in range(NX):
            for lo in range(2):
                parts[pl.ds((r * PQ + lo * 8) * NB + b, 8, stride=NB), :] = tiles[r][:, lo * NQ : (lo + 1) * NQ]
        return carry

    def remote(src, dst, send, recv, to):
        return pltpu.make_async_remote_copy(
            src_ref=src, dst_ref=dst, send_sem=send, recv_sem=recv, device_id=to, device_id_type=MESH
        )

    parts4 = parts.reshape(NX, PQ, NB, NQ)

    def span(g, k):
        n = NB // CHUNKS[g]
        return pl.ds(pl.multiple_of(k * n, n), n)

    def halves(g):
        p0, n = GROUPS[g]
        return pl.ds(p0, n // 2), pl.ds(p0 + n // 2, n // 2)

    def x_copy(g, i, k):
        at = span(g, k)
        lo, hi = halves(g)
        src, dst, to = {
            0: ((x_opp, lo, at), rxo.at[lo, at], right_x),
            1: ((x_opp, hi, at), rxo.at[hi, at], left_x),
            2: ((x_r, hi, at), rxn.at[0, hi, at], right_x),
            3: ((x_l, lo, at), rxn.at[1, lo, at], left_x),
            4: ((x_r, lo, at), rxn.at[0, lo, at], right_x),
            5: ((x_l, hi, at), rxn.at[1, hi, at], left_x),
        }[i]
        return remote(parts4.at[src], dst, xs.at[g, i, k], xr.at[g, i, k], to)

    def x_first(g, k):
        for i in range(4):
            x_copy(g, i, k).start()

    def x_second(g, k):
        at = span(g, k)
        lo, hi = halves(g)
        x_copy(g, 0, k).wait_recv()
        parts4[x_r, lo, at] += rxo[lo, at]
        x_copy(g, 4, k).start()
        x_copy(g, 1, k).wait_recv()
        parts4[x_l, hi, at] += rxo[hi, at]
        x_copy(g, 5, k).start()

    def core_copy(g):
        ps = pl.ds(*GROUPS[g])
        return remote(parts4.at[red, ps], coreacc.at[ps], cs.at[g], cr.at[g], other)

    def x_last(g):
        def one(k, carry):
            for i in (2, 3, 4, 5):
                x_copy(g, i, k).wait_recv()
            return carry

        lax.fori_loop(0, CHUNKS[g], one, 0)
        ps = pl.ds(*GROUPS[g])
        parts4[red, ps] += rxn[0, ps] + rxn[1, ps]
        core_copy(g).start()

    def compute(t):
        ints_copy(t).wait()
        sides(t)
        lax.fori_loop(0, CB, lambda i, carry: block_step(t * CB + i, carry), 0, unroll=CB)

    loads[2].wait()
    loads[3].wait()
    for k in range(1, NCH):
        ints_copy(k).start()
    compute(0)
    pl.semaphore_wait(barrier, len(peers))
    key_copy = remote(kown, koth, ks.at[0], kr.at[0], other)
    key_copy.start()
    x_first(0, 0)

    def chunk_step(t, carry):
        compute(t)
        x_first(0, t)

        @pl.when(t >= 2)
        def _():
            x_second(0, t - 2)

        @pl.when(t % 2 == 1)
        def _():
            x_first(1, t // 2)

        return carry

    lax.fori_loop(1, NCH, chunk_step, 0)

    def many(g, first, last):
        def one(k, carry):
            x_second(g, k)
            return carry

        lax.fori_loop(first, last, one, 0)

    key_copy.wait()
    lane = lax.broadcasted_iota(jnp.int32, (1, 2 * NB), 1)
    both_keys = jnp.where(lane < NB, kown[0:1, :], koth[0:1, :])
    row = lax.broadcasted_iota(jnp.int32, (NY * KEYS, 2 * NB), 0)
    ry, rz, rs = row // KEYS, (row // SLOTS) % NZ, row % SLOTS
    code = (((rz * NY) + ry) * 2 + core) * SLOTS + rs
    place = (code == both_keys).astype(F32).astype(BF)
    place2 = jnp.concatenate([place, place], axis=1)

    def y_copy(g, h):
        ps = pl.ds(*GROUPS[g])
        yy = lax.rem(y + h, NY)
        return remote(dense.at[ps, yy], ryn.at[y, ps], ys.at[g, h], yr.at[g, y], dev(z, yy, core, red))

    def y_wait(g, h):
        ps = pl.ds(*GROUPS[g])
        yy = lax.rem(y + h, NY)
        remote(dense.at[ps, yy], ryn.at[yy, ps], ys.at[g, h], yr.at[g, yy], other).wait_recv()

    def densify(g):
        p0, n = GROUPS[g]
        core_copy(g).wait_recv()
        for p in range(p0, p0 + n, 2):
            own = jnp.concatenate([parts4[red, p], parts4[red, p + 1]], axis=1)
            oth = jnp.concatenate([coreacc[p], coreacc[p + 1]], axis=1)
            both = jnp.concatenate([own, oth], axis=0)
            high = both.astype(BF)
            rest = (both - high.astype(F32)).astype(BF)
            d = jnp.dot(place2, jnp.concatenate([high, rest], axis=0), preferred_element_type=F32)
            dense[p] = d[:, :NQ].reshape(NY, KEYS, NQ)
            dense[p + 1] = d[:, NQ:].reshape(NY, KEYS, NQ)
        for h in range(1, NY):
            y_copy(g, h).start()

    def z_rows(g):
        p0, n = GROUPS[g]
        return pl.ds(p0 * SLOTS, n * SLOTS)

    def z_copy(g, h):
        zz = lax.rem(z + h, NZ)
        at = z_rows(g)
        return remote(zbuf.at[zz, at], zrecv.at[z, at], zs.at[g, h], zr.at[g, z], dev(zz, y, core, red))

    def z_wait(g, h):
        zz = lax.rem(z + h, NZ)
        at = z_rows(g)
        remote(zbuf.at[zz, at], zrecv.at[zz, at], zs.at[g, h], zr.at[g, zz], other).wait_recv()

    zflat = zbuf.reshape(NZ * SLOTS * PQ, NQ)

    def y_last(g):
        p0, n = GROUPS[g]
        for h in range(1, NY):
            y_wait(g, h)
        for i in range(n):
            p = p0 + i
            total = dense[p, y]
            for h in range(1, NY):
                total = total + ryn[lax.rem(y + h, NY), p]
            for zz in range(NZ):
                zflat[pl.ds(zz * SLOTS * PQ + p0 * SLOTS + i, SLOTS, stride=n), :] = total[zz * SLOTS : (zz + 1) * SLOTS]
        for h in range(1, NZ):
            z_copy(g, h).start()

    def z_last(g):
        p0, n = GROUPS[g]
        for h in range(1, NZ):
            z_wait(g, h)
        at = z_rows(g)
        total = zbuf[z, at]
        for h in range(1, NZ):
            total = total + zrecv[lax.rem(z + h, NZ), at]
        lo, i0 = p0 // 8, p0 % 8
        for slot in range(SLOTS):
            outf[pl.ds(slot * PQ + 2 * i0 + lo, n, stride=2), :] = total[slot * n : (slot + 1) * n]

    def x_sent(g):
        def one(k, carry):
            for i in range(6):
                x_copy(g, i, k).wait_send()
            return carry

        lax.fori_loop(0, CHUNKS[g], one, 0)
        core_copy(g).wait_send()

    many(0, NCH - 2, NCH)
    x_first(2, 0)
    many(1, 0, CHUNKS[1])
    x_last(0)
    densify(0)
    x_second(2, 0)
    x_last(1)
    densify(1)
    y_last(0)
    x_sent(0)
    x_last(2)
    densify(2)
    x_sent(1)
    x_sent(2)
    y_last(1)
    z_last(0)
    y_last(2)
    z_last(1)
    z_last(2)
    out_ref[...] = outf[...].astype(BF).reshape(SLOTS, PQ, NQ)

    for g in range(NG):
        for h in range(1, NY):
            y_copy(g, h).wait_send()
        for h in range(1, NZ):
            z_copy(g, h).wait_send()


def shards(
    ints, block_pairs, block_dest, block_slot, occ_density, virt_density, isdf_cols, slab_cols
):
    hbm = pl.BlockSpec(memory_space=pl.ANY)
    vmem = pl.BlockSpec(memory_space=pltpu.VMEM)
    smem = pl.BlockSpec(memory_space=pltpu.SMEM)
    dma = pltpu.SemaphoreType.DMA
    pairs_t = block_pairs.T
    return pl.pallas_call(
        kernel,
        out_shape=jax.ShapeDtypeStruct((SLOTS, PQ, NQ), BF),
        in_specs=[hbm, smem, vmem, vmem, vmem, vmem, hbm, hbm, hbm],
        out_specs=vmem,
        scratch_shapes=[
            pltpu.VMEM((NB, LAM, BA * BA), BF),
            pltpu.VMEM((BA * BA, NAB), BF),
            pltpu.VMEM((LAM * BA, NAB), BF),
            pltpu.VMEM((NAB, BA, NCAND), BF),
            pltpu.VMEM((NB, BA * BA), F32),
            pltpu.VMEM((NB, LAM * BA), F32),
            pltpu.VMEM((CB * BA, 2 * BA), F32),
            pltpu.VMEM((CB * LAM, 2 * BA), F32),
            pltpu.VMEM((NB, 2 * BA, 2 * NQ), BF),
            pltpu.VMEM((NB, LAM, NQ), F32),
            pltpu.VMEM((NX * PQ * NB, NQ), F32),
            pltpu.VMEM((PQ, NB, NQ), F32),
            pltpu.VMEM((2, PQ, NB, NQ), F32),
            pltpu.VMEM((8, 128), jnp.int32),
            pltpu.VMEM((8, 128), jnp.int32),
            pltpu.VMEM((PQ, NB, NQ), F32),
            pltpu.VMEM((PQ, NY, KEYS, NQ), F32),
            pltpu.VMEM((NY, PQ, KEYS, NQ), F32),
            pltpu.VMEM((NZ, SLOTS * PQ, NQ), F32),
            pltpu.VMEM((NZ, SLOTS * PQ, NQ), F32),
            pltpu.VMEM((SLOTS * PQ, NQ), F32),
            dma((4,)),
            dma((NCH,)),
            dma((NG, 6, NCH)),
            dma((NG, 6, NCH)),
            dma((NG,)),
            dma((NG,)),
            dma((1,)),
            dma((1,)),
            dma((NG, NY)),
            dma((NG, NY)),
            dma((NG, NZ)),
            dma((NG, NZ)),
        ],
        compiler_params=pltpu.CompilerParams(
            collective_id=0, has_side_effects=True, vmem_limit_bytes=56 * 1024 * 1024
        ),
        cost_estimate=pl.CostEstimate(flops=3_000_000_000, bytes_accessed=14_000_000, transcendentals=0),
    )(
        ints,
        pairs_t,
        pairs_t,
        block_dest.reshape(1, NB),
        block_slot.reshape(1, NB),
        slab_cols.reshape(1, NQ),
        occ_density.transpose(1, 2, 0).reshape(BA * BA, NAB),
        virt_density.transpose(1, 2, 0).reshape(BA * BA, NAB),
        isdf_cols,
    )


def solution(mesh):
    return jax.shard_map(
        shards,
        mesh=mesh,
        in_specs=(
            P("pair", "red", None),
            P("pair", None),
            P("pair", None),
            P("pair"),
            P(),
            P(),
            P(),
            P(),
        ),
        out_specs=P("pair", "red", None),
        check_vma=False,
    )
```

time: 75 us -> 54.5 us (0.73)
  Pallas kernels: 73.2 us -> 53 us
    pallas_call x1, Pallas kernels: 73.2 us -> 53 us  [shards(): pl.pallas_call(kernel, out_shape=jax.ShapeDtypeStruct((SLOTS, PQ, NQ), BF...]
where the time goes in v2:
time: 54.5 us; the launch traced here: 54.3 us
  Pallas kernels  53 us (97%)
  local copies, waits for them, and re-layouts  1.32 us (2%)
    pallas_call x1, Pallas kernels, shards(): pl.pallas_call(kernel, out_shape=jax.ShapeDtypeStruct((SLOTS, PQ, NQ), BF...  53 us
    unnamed x1, local copies, waits for them, and re-layouts  1.32 us

profile of v2, /device:TPU:2, one launch (start us, length us, event | category | flops | bytes accessed | tf_op | source)
XLA Modules:
  0.0 54.3 jit_solution(7023863592367611154)
XLA Ops:
  0.0 53.0 %shard_map.82 = bf16[4,16,128]{2,1,0:T(8,128)(2,1)} custom-call(bf16[64,16,4096]{2,1,0:T(8,128)(2,1)} %ints_hbm.1, s32[2,64]{1,0:T(2,128)} %bitcast.12, s32[2,64]{1,0:T(2,128)} %bitcast.13, s32[1,64]{1,0:T(1,128)} %bitcast.14, s32[1,64]{1,0:T(1,128)} %bitcast.15, s32[1,128]{1,0:T(1,128)} %bitcast.16, bf16[4096,96]{1,0:T(8,128)(2,1)} %bitcast.10, ...), custom_call_target="tpu_custom_call" | custom-call | flops 3000000000 | bytes 14000000 | tf_op jit(solution)/shard_map/pallas_call | solution.py:360
  53.0 1.3 %copy.10 = bf16[4,16,128]{2,1,0:T(8,128)(2,1)} copy(bf16[4,16,128]{2,1,0:T(8,128)(2,1)} %shard_map.82) | data formatting | bytes 32768

commit v3 on v2

--- a/solution.py
+++ b/solution.py
@@ -23,16 +23,17 @@
 NCH = NB // CB
 GROUPS = ((0, 8), (8, 4), (12, 4))
 NG = len(GROUPS)
+RELAYED = (True, False, False)
 CHUNKS = (8, 4, 1)
 KEYS = NZ * SLOTS
 
 
 def kernel(
-    ints_hbm, pairs_smem, pairs_ref, dest_ref, slot_ref, slab_ref, occ_hbm, virt_hbm, isdf_hbm,
+    ints_hbm, pairs_hbm, dest_hbm, slot_hbm, slab_hbm, occ_hbm, virt_hbm, isdf_hbm,
     out_ref,
-    ints, occ_t, virt_t, isdf, dflat, vflat, dens, vdens, wbd, vside,
-    parts, rxo, rxn, kown, koth, coreacc, dense, ryn, zbuf, zrecv, outf,
-    load_sem, ints_sem, xs, xr, cs, cr, ks, kr, ys, yr, zs, zr,
+    pairs_smem, pairs_ref, dest_ref, slot_ref, slab_ref, ints, occ_t, virt_t, isdf, dflat, vflat, dens, vdens, wbd, vside,
+    parts, rxo, rxn, kown, koth, coreacc, dense, ryo, ryn, ryd, zbuf, zrecv, outf,
+    small_sem, load_sem, ints_sem, xs, xr, cs, cr, ks, kr, ys, yr, zs, zr,
 ):
     pair = lax.axis_index("pair")
     red = lax.axis_index("red")
@@ -43,10 +44,26 @@
     def dev(zz, yy, cc, rr):
         return ((zz * NY + yy) * 2 + cc, rr)
 
+    y_opp, y_r, y_l = lax.rem(y + 2, NY), lax.rem(y + 1, NY), lax.rem(y + 3, NY)
     x_opp, x_r, x_l = lax.rem(red + 2, NX), lax.rem(red + 1, NX), lax.rem(red + 3, NX)
     right_x, left_x = dev(z, y, core, x_r), dev(z, y, core, x_l)
+    right_y, left_y = dev(z, y_r, core, red), dev(z, y_l, core, red)
     other = dev(z, y, 1 - core, red)
 
+    small = [
+        pltpu.make_async_copy(src, dst, small_sem.at[i])
+        for i, (src, dst) in enumerate(
+            (
+                (pairs_hbm, pairs_ref),
+                (slab_hbm, slab_ref),
+                (dest_hbm, dest_ref),
+                (slot_hbm, slot_ref),
+                (pairs_hbm, pairs_smem),
+            )
+        )
+    ]
+    for c in small:
+        c.start()
     half = NAB // 2
     loads = [
         pltpu.make_async_copy(virt_hbm.at[pl.ds(red * (LAM * BA), LAM * BA)], virt_t, load_sem.at[0]),
@@ -65,12 +82,13 @@
     ints_copy(0).start()
 
     barrier = pltpu.get_barrier_semaphore()
-    peers = [right_x, left_x, other]
-    peers += [dev(z, lax.rem(y + h, NY), core, red) for h in range(1, NY)]
+    peers = [right_x, left_x, right_y, left_y, dev(z, y_opp, core, red), other]
     peers += [dev(lax.rem(z + h, NZ), y, core, red) for h in range(1, NZ)]
     for d in peers:
         pl.semaphore_signal(barrier, inc=1, device_id=d, device_id_type=MESH)
 
+    for c in small:
+        c.wait()
     pick = (lax.broadcasted_iota(jnp.int32, (NCAND, NQ), 0) == slab_ref[...]).astype(F32).astype(BF)
 
     def one_hot_rows(row):
@@ -245,15 +263,40 @@
     place = (code == both_keys).astype(F32).astype(BF)
     place2 = jnp.concatenate([place, place], axis=1)
 
-    def y_copy(g, h):
+    def y_halves(g):
+        p0, n = GROUPS[g]
+        return pl.ds(p0, n // 2), pl.ds(p0 + n // 2, n // 2)
+
+    def y_copy(g, i):
+        lo, hi = y_halves(g)
+        src, dst, to = {
+            0: ((lo, y_opp), ryo.at[lo], right_y),
+            1: ((hi, y_opp), ryo.at[hi], left_y),
+            2: ((hi, y_r), ryn.at[0, hi], right_y),
+            3: ((lo, y_l), ryn.at[1, lo], left_y),
+            4: ((lo, y_r), ryn.at[0, lo], right_y),
+            5: ((hi, y_l), ryn.at[1, hi], left_y),
+        }[i]
+        return remote(dense.at[src], dst, ys.at[g, i], yr.at[g, i], to)
+
+    def y_direct(g, h):
         ps = pl.ds(*GROUPS[g])
         yy = lax.rem(y + h, NY)
-        return remote(dense.at[ps, yy], ryn.at[y, ps], ys.at[g, h], yr.at[g, y], dev(z, yy, core, red))
-
-    def y_wait(g, h):
-        ps = pl.ds(*GROUPS[g])
-        yy = lax.rem(y + h, NY)
-        remote(dense.at[ps, yy], ryn.at[yy, ps], ys.at[g, h], yr.at[g, yy], other).wait_recv()
+        return remote(dense.at[ps, yy], ryd.at[h - 1, ps], ys.at[g, h], yr.at[g, h], dev(z, yy, core, red))
+
+    def y_copies(g, which):
+        if RELAYED[g]:
+            return [y_copy(g, i) for i in which]
+        return [y_direct(g, h) for h in (2, 1, 3)]
+
+    def y_second(g):
+        lo, hi = y_halves(g)
+        y_copy(g, 0).wait_recv()
+        dense[lo, y_r] += ryo[lo]
+        y_copy(g, 4).start()
+        y_copy(g, 1).wait_recv()
+        dense[hi, y_l] += ryo[hi]
+        y_copy(g, 5).start()
 
     def densify(g):
         p0, n = GROUPS[g]
@@ -267,8 +310,8 @@
             d = jnp.dot(place2, jnp.concatenate([high, rest], axis=0), preferred_element_type=F32)
             dense[p] = d[:, :NQ].reshape(NY, KEYS, NQ)
             dense[p + 1] = d[:, NQ:].reshape(NY, KEYS, NQ)
-        for h in range(1, NY):
-            y_copy(g, h).start()
+        for c in y_copies(g, range(4)):
+            c.start()
 
     def z_rows(g):
         p0, n = GROUPS[g]
@@ -288,16 +331,18 @@
 
     def y_last(g):
         p0, n = GROUPS[g]
-        for h in range(1, NY):
-            y_wait(g, h)
+        for c in y_copies(g, range(2, 6)):
+            c.wait_recv()
         for i in range(n):
             p = p0 + i
             total = dense[p, y]
-            for h in range(1, NY):
-                total = total + ryn[lax.rem(y + h, NY), p]
+            if RELAYED[g]:
+                total = total + (ryn[0, p] + ryn[1, p])
+            else:
+                total = total + (ryd[0, p] + ryd[1, p] + ryd[2, p])
             for zz in range(NZ):
                 zflat[pl.ds(zz * SLOTS * PQ + p0 * SLOTS + i, SLOTS, stride=n), :] = total[zz * SLOTS : (zz + 1) * SLOTS]
-        for h in range(1, NZ):
+        for h in (4, 3, 5, 2, 6, 1, 7):
             z_copy(g, h).start()
 
     def z_last(g):
@@ -327,24 +372,25 @@
     x_last(0)
     densify(0)
     x_second(2, 0)
+    y_second(0)
     x_last(1)
     densify(1)
+    x_last(2)
+    densify(2)
     y_last(0)
     x_sent(0)
-    x_last(2)
-    densify(2)
     x_sent(1)
     x_sent(2)
     y_last(1)
+    y_last(2)
     z_last(0)
-    y_last(2)
     z_last(1)
     z_last(2)
     out_ref[...] = outf[...].astype(BF).reshape(SLOTS, PQ, NQ)
 
     for g in range(NG):
-        for h in range(1, NY):
-            y_copy(g, h).wait_send()
+        for c in y_copies(g, range(6)):
+            c.wait_send()
         for h in range(1, NZ):
             z_copy(g, h).wait_send()
 
@@ -354,15 +400,19 @@
 ):
     hbm = pl.BlockSpec(memory_space=pl.ANY)
     vmem = pl.BlockSpec(memory_space=pltpu.VMEM)
-    smem = pl.BlockSpec(memory_space=pltpu.SMEM)
     dma = pltpu.SemaphoreType.DMA
     pairs_t = block_pairs.T
     return pl.pallas_call(
         kernel,
         out_shape=jax.ShapeDtypeStruct((SLOTS, PQ, NQ), BF),
-        in_specs=[hbm, smem, vmem, vmem, vmem, vmem, hbm, hbm, hbm],
+        in_specs=[hbm] * 8,
         out_specs=vmem,
         scratch_shapes=[
+            pltpu.SMEM((2, NB), jnp.int32),
+            pltpu.VMEM((2, NB), jnp.int32),
+            pltpu.VMEM((1, NB), jnp.int32),
+            pltpu.VMEM((1, NB), jnp.int32),
+            pltpu.VMEM((1, NQ), jnp.int32),
             pltpu.VMEM((NB, LAM, BA * BA), BF),
             pltpu.VMEM((BA * BA, NAB), BF),
             pltpu.VMEM((LAM * BA, NAB), BF),
@@ -380,10 +430,13 @@
             pltpu.VMEM((8, 128), jnp.int32),
             pltpu.VMEM((PQ, NB, NQ), F32),
             pltpu.VMEM((PQ, NY, KEYS, NQ), F32),
-            pltpu.VMEM((NY, PQ, KEYS, NQ), F32),
+            pltpu.VMEM((PQ, KEYS, NQ), F32),
+            pltpu.VMEM((2, PQ, KEYS, NQ), F32),
+            pltpu.VMEM((NY - 1, PQ, KEYS, NQ), F32),
             pltpu.VMEM((NZ, SLOTS * PQ, NQ), F32),
             pltpu.VMEM((NZ, SLOTS * PQ, NQ), F32),
             pltpu.VMEM((SLOTS * PQ, NQ), F32),
+            dma((5,)),
             dma((4,)),
             dma((NCH,)),
             dma((NG, 6, NCH)),
@@ -392,8 +445,8 @@
             dma((NG,)),
             dma((1,)),
             dma((1,)),
-            dma((NG, NY)),
-            dma((NG, NY)),
+            dma((NG, 6)),
+            dma((NG, 6)),
             dma((NG, NZ)),
             dma((NG, NZ)),
         ],
@@ -403,7 +456,6 @@
         cost_estimate=pl.CostEstimate(flops=3_000_000_000, bytes_accessed=14_000_000, transcendentals=0),
     )(
         ints,
-        pairs_t,
         pairs_t,
         block_dest.reshape(1, NB),
         block_slot.reshape(1, NB),

time: 54.5 us -> 51.6 us (0.947)
  Pallas kernels: 53 us -> 50.1 us
    pallas_call x1, Pallas kernels: 53 us -> 50.1 us  [shards(): pl.pallas_call(kernel, out_shape=jax.ShapeDtypeStruct((SLOTS, PQ, NQ), BF...]
where the time goes in v3:
time: 51.6 us; the launch traced here: 51.4 us
  Pallas kernels  50.1 us (97%)
  local copies, waits for them, and re-layouts  1.32 us (3%)
    pallas_call x1, Pallas kernels, shards(): pl.pallas_call(kernel, out_shape=jax.ShapeDtypeStruct((SLOTS, PQ, NQ), BF...  50.1 us
    unnamed x1, local copies, waits for them, and re-layouts  1.32 us

profile of v3, /device:TPU:2, one launch (start us, length us, event | category | flops | bytes accessed | tf_op | source)
XLA Modules:
  0.0 51.4 jit_solution(3126708252368424590)
XLA Ops:
  0.0 50.1 %shard_map.82 = bf16[4,16,128]{2,1,0:T(8,128)(2,1)} custom-call(bf16[64,16,4096]{2,1,0:T(8,128)(2,1)} %ints_hbm.1, s32[2,64]{1,0:T(2,128)} %bitcast.12, s32[1,64]{1,0:T(1,128)} %bitcast.13, s32[1,64]{1,0:T(1,128)} %bitcast.14, s32[1,128]{1,0:T(1,128)} %bitcast.15, bf16[4096,96]{1,0:T(8,128)(2,1)} %bitcast.10, bf16[4096,96]{1,0:T(8,128)(2,1)} %bitcast.11, ...), custom_call_target="tpu_custom_call" | custom-call | flops 3000000000 | bytes 14000000 | tf_op jit(solution)/shard_map/pallas_call | solution.py:405
  50.1 1.3 %copy.10 = bf16[4,16,128]{2,1,0:T(8,128)(2,1)} copy(bf16[4,16,128]{2,1,0:T(8,128)(2,1)} %shard_map.82) | data formatting | bytes 32768

commit v4 on v3

--- a/solution.py
+++ b/solution.py
@@ -33,7 +33,7 @@
     out_ref,
     pairs_smem, pairs_ref, dest_ref, slot_ref, slab_ref, ints, occ_t, virt_t, isdf, dflat, vflat, dens, vdens, wbd, vside,
     parts, rxo, rxn, kown, koth, coreacc, dense, ryo, ryn, ryd, zbuf, zrecv, outf,
-    small_sem, load_sem, ints_sem, xs, xr, cs, cr, ks, kr, ys, yr, zs, zr,
+    small_sem, load_sem, ints_sem, xs, xr, xl, cs, cr, ks, kr, ys, yr, zs, zr,
 ):
     pair = lax.axis_index("pair")
     red = lax.axis_index("red")
@@ -185,7 +185,8 @@
             4: ((x_r, lo, at), rxn.at[0, lo, at], right_x),
             5: ((x_l, hi, at), rxn.at[1, hi, at], left_x),
         }[i]
-        return remote(parts4.at[src], dst, xs.at[g, i, k], xr.at[g, i, k], to)
+        recv = xr.at[i * sum(CHUNKS) + sum(CHUNKS[:g]) + k] if i < 2 else xl.at[g]
+        return remote(parts4.at[src], dst, xs.at[g], recv, to)
 
     def x_first(g, k):
         for i in range(4):
@@ -206,12 +207,8 @@
         return remote(parts4.at[red, ps], coreacc.at[ps], cs.at[g], cr.at[g], other)
 
     def x_last(g):
-        def one(k, carry):
-            for i in (2, 3, 4, 5):
-                x_copy(g, i, k).wait_recv()
-            return carry
-
-        lax.fori_loop(0, CHUNKS[g], one, 0)
+        late = rxn.at[:, pl.ds(*GROUPS[g])]
+        remote(late, late, xs.at[g], xl.at[g], other).wait_recv()
         ps = pl.ds(*GROUPS[g])
         parts4[red, ps] += rxn[0, ps] + rxn[1, ps]
         core_copy(g).start()
@@ -277,12 +274,12 @@
             4: ((lo, y_r), ryn.at[0, lo], right_y),
             5: ((hi, y_l), ryn.at[1, hi], left_y),
         }[i]
-        return remote(dense.at[src], dst, ys.at[g, i], yr.at[g, i], to)
+        return remote(dense.at[src], dst, ys.at[g], yr.at[g, i if i < 2 else 2], to)
 
     def y_direct(g, h):
         ps = pl.ds(*GROUPS[g])
         yy = lax.rem(y + h, NY)
-        return remote(dense.at[ps, yy], ryd.at[h - 1, ps], ys.at[g, h], yr.at[g, h], dev(z, yy, core, red))
+        return remote(dense.at[ps, yy], ryd.at[h - 1, ps], ys.at[g], yr.at[g, 2], dev(z, yy, core, red))
 
     def y_copies(g, which):
         if RELAYED[g]:
@@ -320,19 +317,18 @@
     def z_copy(g, h):
         zz = lax.rem(z + h, NZ)
         at = z_rows(g)
-        return remote(zbuf.at[zz, at], zrecv.at[z, at], zs.at[g, h], zr.at[g, z], dev(zz, y, core, red))
-
-    def z_wait(g, h):
-        zz = lax.rem(z + h, NZ)
-        at = z_rows(g)
-        remote(zbuf.at[zz, at], zrecv.at[zz, at], zs.at[g, h], zr.at[g, zz], other).wait_recv()
+        return remote(zbuf.at[zz, at], zrecv.at[z, at], zs.at[g], zr.at[g], dev(zz, y, core, red))
+
+    def z_all(g):
+        every = zrecv.at[pl.ds(0, NZ - 1), z_rows(g)]
+        return remote(every, every, zs.at[g], zr.at[g], other)
 
     zflat = zbuf.reshape(NZ * SLOTS * PQ, NQ)
 
     def y_last(g):
         p0, n = GROUPS[g]
-        for c in y_copies(g, range(2, 6)):
-            c.wait_recv()
+        late = (ryn if RELAYED[g] else ryd).at[:, pl.ds(p0, n)]
+        remote(late, late, ys.at[g], yr.at[g, 2], other).wait_recv()
         for i in range(n):
             p = p0 + i
             total = dense[p, y]
@@ -347,8 +343,7 @@
 
     def z_last(g):
         p0, n = GROUPS[g]
-        for h in range(1, NZ):
-            z_wait(g, h)
+        z_all(g).wait_recv()
         at = z_rows(g)
         total = zbuf[z, at]
         for h in range(1, NZ):
@@ -358,12 +353,8 @@
             outf[pl.ds(slot * PQ + 2 * i0 + lo, n, stride=2), :] = total[slot * n : (slot + 1) * n]
 
     def x_sent(g):
-        def one(k, carry):
-            for i in range(6):
-                x_copy(g, i, k).wait_send()
-            return carry
-
-        lax.fori_loop(0, CHUNKS[g], one, 0)
+        sent = parts4.at[pl.ds(0, 3), pl.ds(*GROUPS[g])]
+        remote(sent, sent, xs.at[g], xl.at[g], other).wait_send()
         core_copy(g).wait_send()
 
     many(0, NCH - 2, NCH)
@@ -389,10 +380,9 @@
     out_ref[...] = outf[...].astype(BF).reshape(SLOTS, PQ, NQ)
 
     for g in range(NG):
-        for c in y_copies(g, range(6)):
-            c.wait_send()
-        for h in range(1, NZ):
-            z_copy(g, h).wait_send()
+        sent = dense.at[pl.ds(*GROUPS[g]), pl.ds(0, 3)]
+        remote(sent, sent, ys.at[g], yr.at[g, 2], other).wait_send()
+        z_all(g).wait_send()
 
 
 def shards(
@@ -439,16 +429,17 @@
             dma((5,)),
             dma((4,)),
             dma((NCH,)),
-            dma((NG, 6, NCH)),
-            dma((NG, 6, NCH)),
+            dma((NG,)),
+            dma((2 * sum(CHUNKS),)),
+            dma((NG,)),
             dma((NG,)),
             dma((NG,)),
             dma((1,)),
             dma((1,)),
-            dma((NG, 6)),
-            dma((NG, 6)),
-            dma((NG, NZ)),
-            dma((NG, NZ)),
+            dma((NG,)),
+            dma((NG, 3)),
+            dma((NG,)),
+            dma((NG,)),
         ],
         compiler_params=pltpu.CompilerParams(
             collective_id=0, has_side_effects=True, vmem_limit_bytes=56 * 1024 * 1024

time: 51.6 us -> 48.7 us (0.944)
  Pallas kernels: 50.1 us -> 47.1 us
    pallas_call x1, Pallas kernels: 50.1 us -> 47.1 us  [shards(): pl.pallas_call(kernel, out_shape=jax.ShapeDtypeStruct((SLOTS, PQ, NQ), BF...]
where the time goes in v4:
time: 48.7 us; the launch traced here: 48.5 us
  Pallas kernels  47.1 us (97%)
  local copies, waits for them, and re-layouts  1.32 us (3%)
    pallas_call x1, Pallas kernels, shards(): pl.pallas_call(kernel, out_shape=jax.ShapeDtypeStruct((SLOTS, PQ, NQ), BF...  47.1 us
    unnamed x1, local copies, waits for them, and re-layouts  1.32 us

profile of v4, /device:TPU:2, one launch (start us, length us, event | category | flops | bytes accessed | tf_op | source)
XLA Modules:
  0.0 48.5 jit_solution(8264865940160181616)
XLA Ops:
  0.0 47.1 %shard_map.82 = bf16[4,16,128]{2,1,0:T(8,128)(2,1)} custom-call(bf16[64,16,4096]{2,1,0:T(8,128)(2,1)} %ints_hbm.1, s32[2,64]{1,0:T(2,128)} %bitcast.12, s32[1,64]{1,0:T(1,128)} %bitcast.13, s32[1,64]{1,0:T(1,128)} %bitcast.14, s32[1,128]{1,0:T(1,128)} %bitcast.15, bf16[4096,96]{1,0:T(8,128)(2,1)} %bitcast.10, bf16[4096,96]{1,0:T(8,128)(2,1)} %bitcast.11, ...), custom_call_target="tpu_custom_call" | custom-call | flops 3000000000 | bytes 14000000 | tf_op jit(solution)/shard_map/pallas_call | solution.py:395
  47.2 1.3 %copy.10 = bf16[4,16,128]{2,1,0:T(8,128)(2,1)} copy(bf16[4,16,128]{2,1,0:T(8,128)(2,1)} %shard_map.82) | data formatting | bytes 32768

commit v5 on v4

--- a/solution.py
+++ b/solution.py
@@ -232,9 +232,9 @@
         compute(t)
         x_first(0, t)
 
-        @pl.when(t >= 2)
+        @pl.when(t >= 3)
         def _():
-            x_second(0, t - 2)
+            x_second(0, t - 3)
 
         @pl.when(t % 2 == 1)
         def _():
@@ -357,7 +357,7 @@
         remote(sent, sent, xs.at[g], xl.at[g], other).wait_send()
         core_copy(g).wait_send()
 
-    many(0, NCH - 2, NCH)
+    many(0, NCH - 3, NCH)
     x_first(2, 0)
     many(1, 0, CHUNKS[1])
     x_last(0)

time: 48.7 us -> 48.2 us (0.990)
  Pallas kernels: 47.1 us -> 46.5 us
    pallas_call x1, Pallas kernels: 47.1 us -> 46.5 us  [shards(): pl.pallas_call(kernel, out_shape=jax.ShapeDtypeStruct((SLOTS, PQ, NQ), BF...]
where the time goes in v5:
time: 48.2 us; the launch traced here: 47.8 us
  Pallas kernels  46.5 us (96%)
  local copies, waits for them, and re-layouts  1.32 us (3%)
    pallas_call x1, Pallas kernels, shards(): pl.pallas_call(kernel, out_shape=jax.ShapeDtypeStruct((SLOTS, PQ, NQ), BF...  46.5 us
    unnamed x1, local copies, waits for them, and re-layouts  1.32 us

profile of v5, /device:TPU:2, one launch (start us, length us, event | category | flops | bytes accessed | tf_op | source)
XLA Modules:
  0.0 47.8 jit_solution(11095192478396320478)
XLA Ops:
  0.0 46.5 %shard_map.82 = bf16[4,16,128]{2,1,0:T(8,128)(2,1)} custom-call(bf16[64,16,4096]{2,1,0:T(8,128)(2,1)} %ints_hbm.1, s32[2,64]{1,0:T(2,128)} %bitcast.12, s32[1,64]{1,0:T(1,128)} %bitcast.13, s32[1,64]{1,0:T(1,128)} %bitcast.14, s32[1,128]{1,0:T(1,128)} %bitcast.15, bf16[4096,96]{1,0:T(8,128)(2,1)} %bitcast.10, bf16[4096,96]{1,0:T(8,128)(2,1)} %bitcast.11, ...), custom_call_target="tpu_custom_call" | custom-call | flops 3000000000 | bytes 14000000 | tf_op jit(solution)/shard_map/pallas_call | solution.py:395
  46.5 1.3 %copy.10 = bf16[4,16,128]{2,1,0:T(8,128)(2,1)} copy(bf16[4,16,128]{2,1,0:T(8,128)(2,1)} %shard_map.82) | data formatting | bytes 32768
